TPU v7x, 256 devices: a whole 4x4x8 slice. The times are simulated.
256 devices in a mesh: row: 16 (over x, z_lo, core), col: 16 (over z_hi, y).
Axes of the slice: x: 4, y: 4, z: 8 (z_hi: 4, z_lo: 2; z = z_hi * 2 + z_lo), core: 2. Of those that a mesh axis runs over, the one named last changes fastest.
Arguments:
- points: float32 [131072, 32], P(('row', 'col')), may hold values from -6 to 6
- lengthscale: float32 [32], replicated, may hold values from 4 to 32
- weekday: int32 [131072], P(('row', 'col')), may hold values from 0 to 6
- solution: float32 [131072, 32], P(('row', 'col')), may hold values from -6 to 6
- residual: float32 [131072, 32], P(('row', 'col')), may hold values from -70 to 70
- direction: float32 [131072, 32], P(('row', 'col')), may hold values from -70 to 70
Outputs:
- new_solution: float32 [131072, 32], P(('row', 'col'))
- new_residual: float32 [131072, 32], P(('row', 'col'))
- new_direction: float32 [131072, 32], P(('row', 'col'))
All inputs are finite; a program needn't handle non-finite values.
Results may differ from a plain program's by a relative error of at most 0.0068.
Values may be sent and summed in bfloat16 or wider, within the bound.
A program may use at most 64 MiB of HBM per device.

v0:
```python
import jax
import jax.numpy as jnp
from jax import lax
from jax.sharding import PartitionSpec as P

root_five = 2.23606797749979
noise_level = 0.5
cross_day = 0.4


def kernel_values(inner_prod, left_norms, right_norms, same_day):
    squared = jnp.maximum(left_norms + right_norms - 2.0 * inner_prod, 0.0)
    scaled_dist = root_five * jnp.sqrt(squared)
    matern = (1.0 + scaled_dist + 5.0 / 3.0 * squared) * jnp.exp(-scaled_dist)
    return matern * jnp.where(same_day, 1.0, cross_day)


def square_norms(values):
    widened = values.astype(jnp.float32)
    return jnp.sum(widened * widened, axis=-1)


def per_device(points, lengthscale, weekday, solution, residual, direction):
    scaled = (points / lengthscale).astype(jnp.bfloat16)
    day_codes = weekday.astype(jnp.bfloat16)
    half_direction = direction.astype(jnp.bfloat16)
    shard_rows = points.shape[0]
    probes = direction.shape[1]
    count_row = lax.axis_size("row")
    count_col = lax.axis_size("col")
    old_norm = lax.psum(jnp.sum(residual * residual, axis=0), ("row", "col"))
    col_scaled, col_codes, col_steer = (
        lax.all_gather(scaled, "row", axis=0, tiled=True),
        lax.all_gather(day_codes, "row", axis=0, tiled=True),
        lax.all_gather(half_direction, "row", axis=0, tiled=True),
    )
    col_norms = square_norms(col_scaled)
    row_scaled, row_codes, row_steer = (
        lax.all_gather(scaled, "col", axis=0, tiled=True),
        lax.all_gather(day_codes, "col", axis=0, tiled=True),
        lax.all_gather(half_direction, "col", axis=0, tiled=True),
    )
    row_norms = square_norms(row_scaled)
    devices = count_row * count_col
    slot_count = devices // 2
    group_size = 8
    turn_count = slot_count // group_size
    my_row = lax.axis_index("row")
    my_col = lax.axis_index("col")
    candidates = jnp.arange(count_col, dtype=jnp.int32)
    target = (my_col - my_row) % count_col
    quotient = jnp.sum(jnp.where(candidates * (count_row + 1) % count_col == target, candidates, 0))
    myself = quotient * count_row + my_row
    row_blocks = (
        row_scaled.reshape(count_col, shard_rows, -1),
        row_norms.reshape(count_col, shard_rows),
        row_codes.reshape(count_col, shard_rows),
        row_steer.reshape(count_col, shard_rows, probes),
    )
    col_blocks = (
        col_scaled.reshape(count_row, shard_rows, -1),
        col_norms.reshape(count_row, shard_rows),
        col_codes.reshape(count_row, shard_rows),
        col_steer.reshape(count_row, shard_rows, probes),
    )

    def one_turn(turn_index, partial_value):
        row_acc, col_acc = partial_value
        offsets = turn_index * group_size + 1 + jnp.arange(group_size, dtype=jnp.int32)
        partner = (myself + offsets) % devices
        col_pick = partner % count_row
        row_pick = (partner // count_row + partner) % count_col
        kept_share = jnp.where(
            offsets == slot_count, (myself < slot_count).astype(jnp.float32), 1.0
        )
        left_parts = [jnp.take(member, row_pick, axis=0) for member in row_blocks]
        right_parts = [jnp.take(member, col_pick, axis=0) for member in col_blocks]
        inner_prod = jnp.einsum(
            "gpf,gqf->gpq", left_parts[0], right_parts[0], preferred_element_type=jnp.float32
        )
        values = kernel_values(
            inner_prod,
            left_parts[1][:, :, None],
            right_parts[1][:, None, :],
            left_parts[2][:, :, None] == right_parts[2][:, None, :],
        )
        kernel_tile = (values * kept_share[:, None, None]).astype(jnp.bfloat16)
        row_part = jnp.einsum(
            "gpq,gqk->gpk", kernel_tile, right_parts[3], preferred_element_type=jnp.float32
        )
        col_part = jnp.einsum(
            "gpq,gpk->gqk", kernel_tile, left_parts[3], preferred_element_type=jnp.float32
        )
        row_hot = (row_pick[:, None] == jnp.arange(count_col, dtype=jnp.int32)[None, :]).astype(
            jnp.float32
        )
        col_hot = (col_pick[:, None] == jnp.arange(count_row, dtype=jnp.int32)[None, :]).astype(
            jnp.float32
        )
        row_acc = row_acc + jnp.einsum(
            "gi,gpk->ipk", row_hot, row_part, precision=lax.Precision.HIGHEST
        )
        col_acc = col_acc + jnp.einsum(
            "gj,gqk->jqk", col_hot, col_part, precision=lax.Precision.HIGHEST
        )
        return (row_acc, col_acc)

    row_start = jnp.zeros((count_col, shard_rows, probes), jnp.float32)
    col_start = jnp.zeros((count_row, shard_rows, probes), jnp.float32)
    row_acc, col_acc = lax.fori_loop(0, turn_count, one_turn, (row_start, col_start))
    row_partial = row_acc.reshape(count_col * shard_rows, probes)
    col_partial = col_acc.reshape(count_row * shard_rows, probes)
    own_norms = square_norms(scaled)
    own_inner = jnp.einsum("pf,qf->pq", scaled, scaled, preferred_element_type=jnp.float32)
    own_tile = kernel_values(
        own_inner, own_norms[:, None], own_norms[None, :], day_codes[:, None] == day_codes[None, :]
    ).astype(jnp.bfloat16)
    own_part = jnp.dot(own_tile, half_direction, preferred_element_type=jnp.float32)
    row_total = lax.psum_scatter(row_partial, "col", scatter_dimension=0, tiled=True)
    applied = (
        row_total + lax.psum_scatter(col_partial, "row", scatter_dimension=0, tiled=True) + own_part
    )
    image = applied + noise_level * direction
    curvature = lax.psum(jnp.sum(direction * image, axis=0), ("row", "col"))
    step_length = old_norm / curvature
    new_residual = residual - step_length * image
    new_norm = lax.psum(jnp.sum(new_residual * new_residual, axis=0), ("row", "col"))
    new_solution = solution + step_length * direction
    new_direction = new_residual + new_norm / old_norm * direction
    return (new_solution, new_residual, new_direction)


def solution(mesh):
    in_specs = (
        P(("row", "col"), None),
        P(),
        P(("row", "col")),
        P(("row", "col"), None),
        P(("row", "col"), None),
        P(("row", "col"), None),
    )
    out_specs = (P(("row", "col"), None), P(("row", "col"), None), P(("row", "col"), None))
    return jax.shard_map(
        per_device, mesh=mesh, in_specs=in_specs, out_specs=out_specs, check_vma=False
    )
```

profile of v0, /device:TPU:1, one launch (start us, length us, event | category | flops | bytes accessed | tf_op | source)
XLA Modules:
  0.0 1016.4 jit_solution(9384316513043719111)
XLA Ops:
  8.2 43.5 %all_gather.18 = bf16[8192,32]{0,1:T(8,128)(2,1)S(1)} all-gather(bf16[512,32]{0,1:T(8,128)(2,1)S(1)} %get-tuple-element.422), channel_id=1, replica_groups=mesh['row'=16,'col'=16] {'col'}, dimensions={0}, use_global_device_ids=true | all-gather | bytes 557056 | tf_op jit(solution)/shard_map/all_gather | solution.py:39
  51.7 29.9 %all_gather.19 = bf16[8192,32]{0,1:T(8,128)(2,1)S(1)} all-gather(bf16[512,32]{0,1:T(8,128)(2,1)S(1)} %get-tuple-element.422), channel_id=1, replica_groups=mesh['row'=16,'col'=16] {'row'}, dimensions={0}, use_global_device_ids=true | all-gather | bytes 557056 | tf_op jit(solution)/shard_map/all_gather | solution.py:33
  85.4 16.4 %all-gather.1 = bf16[16,1,512]{2,1,0:T(2,128)(2,1)S(1)} all-gather(bf16[1,1,512]{2,1,0:T(2,128)(2,1)S(1)} %reshape.191), channel_id=1, replica_groups=mesh['row'=16,'col'=16] {'row'}, dimensions={0}, use_global_device_ids=true | all-gather | bytes 17408 | tf_op jit(solution)/shard_map/all_gather | solution.py:34
  101.8 31.1 %all-gather = bf16[16,1,512]{2,1,0:T(2,128)(2,1)S(1)} all-gather(bf16[1,1,512]{2,1,0:T(2,128)(2,1)S(1)} %reshape.191), channel_id=1, replica_groups=mesh['row'=16,'col'=16] {'col'}, dimensions={0}, use_global_device_ids=true | all-gather | bytes 17408 | tf_op jit(solution)/shard_map/all_gather | solution.py:40
  133.0 26.9 %all_gather.22 = bf16[8192,32]{0,1:T(8,128)(2,1)S(1)} all-gather(bf16[512,32]{0,1:T(8,128)(2,1)S(1)} %convert_element_type.53), channel_id=1, replica_groups=mesh['row'=16,'col'=16] {'row'}, dimensions={0}, use_global_device_ids=true | all-gather | bytes 557056 | tf_op jit(solution)/shard_map/all_gather | solution.py:35
  159.9 37.4 %all_gather.23 = bf16[8192,32]{0,1:T(8,128)(2,1)S(1)} all-gather(bf16[512,32]{0,1:T(8,128)(2,1)S(1)} %convert_element_type.53), channel_id=1, replica_groups=mesh['row'=16,'col'=16] {'col'}, dimensions={0}, use_global_device_ids=true | all-gather | bytes 557056 | tf_op jit(solution)/shard_map/all_gather | solution.py:41
  202.2 505.4 %while.19 = (s32[]{:T(128)}, f32[16,512,32]{1,0,2:T(8,128)S(1)}, f32[16,512,32]{1,0,2:T(8,128)}, s32[]{:T(128)}, f32[16,512]{1,0:T(8,128)S(1)}, /*index=5*/f32[1...) while((s32[]{:T(128)}, f32[16,512,32]{1,0,2:T(8,128)S(1)}, ...), condition=%wide.region_6.10_spmd.clone, body=%wide.region_5.9_spmd.clone.sunk | while | flops 486034176 | bytes 22274972 | solution.py:110
  209.5 8.5 multiply_convert_fusion.3
  227.8 3.6 fusion.77
  240.0 8.5 multiply_convert_fusion.3
  250.8 3.2 fusion.78
  259.5 3.6 fusion.77
  271.7 8.5 multiply_convert_fusion.3
  282.4 3.2 fusion.78
  291.1 3.6 fusion.77
  303.3 8.5 multiply_convert_fusion.3
  322.8 3.6 fusion.77
  335.0 8.5 multiply_convert_fusion.3
  354.5 3.6 fusion.77
  366.6 8.5 multiply_convert_fusion.3
  386.1 3.6 fusion.77
  398.3 8.5 multiply_convert_fusion.3
  417.8 3.6 fusion.77
  430.0 8.5 multiply_convert_fusion.3
  449.4 3.6 fusion.77
  461.6 8.5 multiply_convert_fusion.3
  472.4 3.2 fusion.78
  481.1 3.6 fusion.77
  493.3 8.5 multiply_convert_fusion.3
  504.1 3.2 fusion.78
  512.8 3.6 fusion.77
  525.0 8.5 multiply_convert_fusion.3
  535.8 3.2 fusion.78
  544.4 3.6 fusion.77
  556.6 8.5 multiply_convert_fusion.3
  576.1 3.6 fusion.77
  588.3 8.5 multiply_convert_fusion.3
  607.8 3.6 fusion.77
  619.9 8.5 multiply_convert_fusion.3
  639.4 3.6 fusion.77
  651.6 8.5 multiply_convert_fusion.3
  671.1 3.6 fusion.77
  683.3 8.5 multiply_convert_fusion.3
  702.7 3.6 fusion.77
  712.3 79.5 %reduce-scatter.3.cloned.1.call-done = f32[512,32]{0,1:T(8,128)} async-done(((f32[8192,32]{0,1:T(8,128)}), f32[512,32]{0,1:T(8,128)}) %reduce-scatter.3.cloned.1.call-update) | async-done | bytes 65552 | tf_op jit(solution)/shard_map/reduce_scatter | solution.py:119
  791.8 63.1 %reduce-scatter.5.cloned.1.call-done = f32[512,32]{0,1:T(8,128)} async-done(((f32[8192,32]{0,1:T(8,128)}), f32[512,32]{0,1:T(8,128)}) %reduce-scatter.5.cloned.1.call-update) | async-done | bytes 65552 | tf_op jit(solution)/shard_map/reduce_scatter | solution.py:121
  856.9 79.2 %all-reduce = (f32[32]{0:T(128)S(1)}, f32[32]{0:T(128)S(1)}) all-reduce(f32[32]{0:T(128)S(1)} %multiply_reduce_fusion.5, f32[32]{0:T(128)S(1)} %get-tuple-element.427), channel_id=1, replica_groups=mesh['row'=16,'col'=16] {'row','col'}, use_global_device_ids=true, to_apply=%region_1.0 | all-reduce | flops 64 | bytes 512 | tf_op jit(solution)/shard_map/psum | solution.py:31
  936.3 72.6 %psum.23 = f32[32]{0:T(128)S(1)} all-reduce(f32[32]{0:T(128)S(1)} %get-tuple-element.419), channel_id=1, replica_groups=mesh['row'=16,'col'=16] {'row','col'}, use_global_device_ids=true, to_apply=%region_13.17 | all-reduce | flops 32 | bytes 256 | tf_op jit(solution)/shard_map/psum | solution.py:127
  (370 shorter events, 312.4 us)
Async XLA Ops:
  7.2 78.2 %copy-start.4 = (s32[512]{0:T(512)S(1)}, s32[512]{0:T(512)}, u32[]{:S(2)}) copy-start(s32[512]{0:T(512)} %param.16) | copy-start | bytes 6148
  7.2 125.8 %copy-start.2 = (f32[512,32]{0,1:T(8,128)S(1)}, f32[512,32]{0,1:T(8,128)}, u32[]{:S(2)}) copy-start(f32[512,32]{0,1:T(8,128)} %param.19) | copy-start | bytes 196612
  7.2 784.6 %reduce-scatter.3.cloned.1.call-start = ((), (), s32[]{:S(2)}) async-start(), calls=%async_computation.2 | async-start | bytes 1114112 | tf_op jit(solution)/shard_map/reduce_scatter | solution.py:119
  707.6 4.6 copy-start.1
  709.2 299.6 %copy-start.3 = (f32[512,32]{0,1:T(8,128)S(1)}, f32[512,32]{0,1:T(8,128)}, u32[]{:S(2)}) copy-start(f32[512,32]{0,1:T(8,128)} %param.17) | copy-start | bytes 196612
  709.2 145.6 %reduce-scatter.5.cloned.1.call-start = ((), (), s32[]{:S(2)}) async-start(), calls=%async_computation.3 | async-start | bytes 1114112 | tf_op jit(solution)/shard_map/reduce_scatter | solution.py:121
  936.3 73.3 %copy-start = (f32[512,32]{0,1:T(8,128)}, f32[512,32]{0,1:T(8,128)S(1)}, u32[]{:S(2)}) copy-start(f32[512,32]{0,1:T(8,128)S(1)} %get-tuple-element.420) | copy-start | bytes 196612
Sparse Core Ops, SparseCore 0:
  709.3 82.4 reduce-scatter.2
  794.4 60.3 reduce-scatter.4
where the time goes:
time: 1020 us
  blocking collectives  337 us (33%)
  matrix products  314 us (31%)
  local copies, waits for them, and re-layouts  197 us (19%)
  waiting for transfers between devices  143 us (14%)
  between operations  14.9 us (1%)
    dot_general x16, matrix products, one_turn(): jnp.einsum('gpf,gqf->gpq', left_parts[0], right_parts[0], preferred_eleme...  135 us
    gather x64, local copies, waits for them, and re-layouts, one_turn(): left_parts = [jnp.take(member, row_pick, axis=0) for member in row_blocks]  93 us
    gather x64, local copies, waits for them, and re-layouts, one_turn(): right_parts = [jnp.take(member, col_pick, axis=0) for member in col_blocks]  92.9 us
    reduce_scatter x1, waiting for transfers between devices, per_device(): lax.psum_scatter(row_partial, 'col', scatter_dimension=0, tiled=True)  79.5 us
    psum x1, blocking collectives, per_device(): old_norm = lax.psum(jnp.sum(residual * residual, axis=0), ('row', 'col'))  79.2 us
    psum x1, blocking collectives, per_device(): lax.psum(jnp.sum(new_residual * new_residual, axis=0), ('row', 'col'))  72.6 us
    reduce_scatter x1, waiting for transfers between devices, per_device(): lax.psum_scatter(col_partial, 'row', scatter_dimension=0, tiled=True)  63.1 us
    dot_general x16, matrix products, one_turn(): jnp.einsum('gpq,gqk->gpk', kernel_tile, right_parts[3], preferred_element...  57 us
  transfers between devices with their start and end apart: 2, of which 2 were waited for; matrix products, arithmetic and copies ran while one was open for 0% of the time, Pallas kernels for 0%

commit v1 on v0

v1 whole, which is shorter than its diff:
```python
import functools

import jax
import jax.numpy as jnp
from jax import lax
from jax.experimental import pallas as pl
from jax.experimental.pallas import tpu as pltpu
from jax.sharding import PartitionSpec as P

f32 = jnp.float32
bf16 = jnp.bfloat16
MESH = pl.DeviceIdType.MESH

root_five = 2.23606797749979
log2_e = 1.4426950408889634
noise_level = 0.5
cross_day = 0.4

MISC = 32
STEER = 48
PACK = 80
GROUP = 16
HALF = 8
OUT_SCALE = 5.0 / 3.0 * cross_day
SAME_DAY = 1.0 / cross_day


def kernel_values(squared, row_days, col_days):
    m = jnp.maximum(squared, 1e-30)
    u = m * lax.rsqrt(m)
    e = jnp.exp2(u * (-root_five * log2_e))
    p = (u + 3.0 / root_five) * u + 0.6
    k = (p * e).astype(bf16)
    return k * jnp.where(row_days == col_days, bf16(SAME_DAY), bf16(1.0))


def step_kernel(
    pts_ref, ls_ref, day_ref, sol_ref, res_ref, dir_ref,
    nsol_ref, nres_ref, ndir_ref,
    gcol, grow, xa, da, k0, k1, ro, co, srow, scol, rrow, rcol, stat, st1, st2,
    gc_send, gc_recv, gr_send, gr_recv, rr_send, rr_recv, rc_send, rc_recv,
    s1_send, s1_recv, s2_send, s2_recv,
):
    r = lax.axis_index("row")
    c = lax.axis_index("col")

    def at_row(d):
        return (lax.rem(r + d, GROUP), c)

    def at_col(d):
        return (r, lax.rem(c + d, GROUP))

    barrier = pltpu.get_barrier_semaphore()

    def greet(d, _):
        pl.semaphore_signal(barrier, inc=1, device_id=at_row(d), device_id_type=MESH)
        pl.semaphore_signal(barrier, inc=1, device_id=at_col(d), device_id_type=MESH)
        return 0

    lax.fori_loop(1, GROUP, greet, 0)

    def gather_col(d):
        return pltpu.make_async_remote_copy(
            src_ref=gcol.at[0], dst_ref=gcol.at[d], send_sem=gc_send.at[d],
            recv_sem=gc_recv.at[d], device_id=at_row(GROUP - d), device_id_type=MESH)

    def gather_row(d):
        return pltpu.make_async_remote_copy(
            src_ref=gcol.at[0], dst_ref=grow.at[d], send_sem=gr_send.at[d],
            recv_sem=gr_recv.at[d], device_id=at_col(GROUP - d), device_id_type=MESH)

    def give_row(d):
        return pltpu.make_async_remote_copy(
            src_ref=srow.at[d], dst_ref=rrow.at[d], send_sem=rr_send.at[d],
            recv_sem=rr_recv.at[d], device_id=at_col(d), device_id_type=MESH)

    def give_col(d):
        return pltpu.make_async_remote_copy(
            src_ref=scol.at[d], dst_ref=rcol.at[d], send_sem=rc_send.at[d],
            recv_sem=rc_recv.at[d], device_id=at_row(d), device_id_type=MESH)

    def share_row(d):
        return pltpu.make_async_remote_copy(
            src_ref=stat.at[0], dst_ref=st1.at[d], send_sem=s1_send.at[d],
            recv_sem=s1_recv.at[d], device_id=at_row(d), device_id_type=MESH)

    def share_col(d):
        return pltpu.make_async_remote_copy(
            src_ref=stat.at[1], dst_ref=st2.at[d], send_sem=s2_send.at[d],
            recv_sem=s2_recv.at[d], device_id=at_col(d), device_id_type=MESH)

    direction = dir_ref[...]
    scales = jnp.transpose(jnp.broadcast_to(ls_ref[...], (128, 32)))[:, :1]
    scaled = (pts_ref[...] / scales).astype(bf16)
    wide = scaled.astype(f32)
    norm = jnp.sum(wide * wide, axis=0, keepdims=True)
    norm_hi = norm.astype(bf16).astype(f32)
    rest = norm - norm_hi
    norm_mid = rest.astype(bf16).astype(f32)
    norm_lo = rest - norm_mid
    points = norm.shape[1]
    line = lax.broadcasted_iota(jnp.int32, (16, points), 0)
    misc = jnp.where(line == 0, norm_hi, 0.0)
    misc = jnp.where(line == 1, norm_mid, misc)
    misc = jnp.where(line == 2, norm_lo, misc)
    misc = jnp.where((line >= 3) & (line < 6), 1.0, misc)
    misc = jnp.where(line == 6, day_ref[...].astype(f32), misc)
    for own in (gcol, grow):
        own[0, :MISC, :] = scaled
        own[0, MISC:STEER, :] = misc.astype(bf16)
        own[0, STEER:, :] = direction.astype(bf16)

    ro[...] = jnp.zeros_like(ro)
    co[...] = jnp.zeros_like(co)

    def prepare(i):
        extra = grow[i, MISC:STEER, :].astype(f32)
        left = jnp.where(line < 3, 1.0, jnp.where(line < 6, pltpu.roll(extra, 3, 0), 0.0))
        block = jnp.concatenate(
            [grow[i, :MISC, :].astype(f32) * -2.0, left, jnp.zeros((128 - STEER, points), f32)], axis=0)
        xa[i] = jnp.transpose(block).astype(bf16)
        da[i] = jnp.transpose(jnp.broadcast_to(extra[6:7, :], (128, points))).astype(bf16)

    def fill(k, i, j):
        squared = jnp.dot(xa[i, :, :STEER], gcol[j, :STEER, :], preferred_element_type=f32)
        days = da[i]
        days = jnp.concatenate([days] * (points // 128), axis=1)
        k[...] = kernel_values(squared, days, gcol[j, MISC + 6:MISC + 7, :])

    def apply(k, i, j, kept):
        row_part = lax.dot_general(
            gcol[j, STEER:, :], k[...], (((1,), (1,)), ((), ())), preferred_element_type=f32)
        col_part = jnp.dot(grow[i, STEER:, :], k[...], preferred_element_type=f32)
        if kept is not None:
            row_part, col_part = row_part * kept, col_part * kept
        ro[i] += row_part
        co[j] += col_part

    def where_is(t):
        return t // GROUP, lax.rem(t, GROUP)

    prepare(0)
    pl.semaphore_wait(barrier, 2 * (GROUP - 1))

    def send_col(n, _):
        gather_col(n).start()
        return 0

    def send_row(n, _):
        gather_row(n).start()
        return 0

    lax.fori_loop(HALF, GROUP, send_col, 0)
    gather_row(1).start()
    lax.fori_loop(1, HALF, send_col, 0)
    lax.fori_loop(2, HALF + 1, send_row, 0)

    fill(k0, 0, 0)
    co[0] = jnp.dot(grow[0, STEER:, :], k0[...], preferred_element_type=f32)

    first, last = HALF, HALF * GROUP + HALF
    row_kept = jnp.where(r < HALF, 1.0, 0.0)
    col_kept = jnp.where(c < HALF, 1.0, 0.0)

    gather_col(HALF).wait_recv()
    fill(k0, 0, HALF)

    def arrive(t):
        i, j = where_is(t)

        @pl.when((t < GROUP) | ((t > GROUP) & (t < 2 * GROUP - HALF)))
        def _():
            gather_col(j).wait_recv()

    def leave(t):
        i, j = where_is(t)

        @pl.when((t > HALF * GROUP - HALF) & (t != HALF * GROUP))
        def _():
            scol[j] = co[j].astype(bf16)
            give_col(j).start()

    def two(m, _):
        t = first + 2 * m
        i0, j0 = where_is(t)
        i1, j1 = where_is(t + 1)
        i2, j2 = where_is(t + 2)
        arrive(t + 1)
        arrive(t + 2)

        @pl.when(j2 == 0)
        def _():
            gather_row(i2).wait_recv()
            prepare(i2)

        kept = jnp.where(t == first, row_kept, jnp.where(t == HALF * GROUP, col_kept, 1.0))
        fill(k1, i1, j1)
        apply(k0, i0, j0, kept)
        fill(k0, i2, j2)
        apply(k1, i1, j1, None)

        leave(t)
        leave(t + 1)

        @pl.when((j1 == GROUP - 1) & (i1 > 0))
        def _():
            srow[i1] = ro[i1].astype(bf16)
            give_row(i1).start()

        return 0

    lax.fori_loop(0, (last - first) // 2, two, 0)
    apply(k0, HALF, HALF, row_kept)
    scol[HALF] = co[HALF].astype(bf16)
    give_col(HALF).start()
    srow[HALF] = ro[HALF].astype(bf16)
    give_row(HALF).start()

    co[0] += ro[0]

    def take_row(d, _):
        give_row(d).wait_recv()
        co[0] += rrow[d].astype(f32)
        return 0

    def take_col(d, _):
        give_col(d).wait_recv()
        co[0] += rcol[d].astype(f32)
        return 0

    lax.fori_loop(1, HALF, take_row, 0)
    lax.fori_loop(HALF + 1, GROUP, take_col, 0)
    lax.fori_loop(1, HALF + 1, take_col, 0)
    take_row(HALF, 0)

    image = co[0] * OUT_SCALE + noise_level * direction
    residual = res_ref[...]
    lane = lax.broadcasted_iota(jnp.int32, (32, 128), 1)
    sums = [residual * residual, direction * image, residual * image, image * image]
    sums = [jnp.sum(v, axis=1, keepdims=True) for v in sums]
    packed = jnp.where(lane == 0, sums[0], jnp.where(lane == 1, sums[1], jnp.where(lane == 2, sums[2], sums[3])))

    def exchange(slot, packed, copy, landing):
        stat[slot] = packed

        def begin(d, _):
            copy(d).start()
            return 0

        def take(d, total):
            copy(d).wait_recv()
            return total + landing[d]

        lax.fori_loop(1, GROUP, begin, 0)
        return lax.fori_loop(1, GROUP, take, packed)

    packed = exchange(0, packed, share_row, st1)
    packed = exchange(1, packed, share_col, st2)
    old_norm, curvature, mixed, image_norm = (packed[:, n:n + 1] for n in range(4))
    step = old_norm / curvature
    new_norm = old_norm - 2.0 * step * mixed + step * step * image_norm
    new_residual = residual - step * image
    nsol_ref[...] = sol_ref[...] + step * direction
    nres_ref[...] = new_residual
    ndir_ref[...] = new_residual + new_norm / old_norm * direction

    def finish(d, _):
        gather_col(d).wait_send()
        give_col(d).wait_send()
        share_row(d).wait_send()
        share_col(d).wait_send()
        return 0

    def finish_row(d, _):
        gather_row(d).wait_send()
        give_row(d).wait_send()
        return 0

    lax.fori_loop(1, GROUP, finish, 0)
    lax.fori_loop(1, HALF + 1, finish_row, 0)


def per_device(points, lengthscale, weekday, solution, residual, direction):
    count, feats = points.shape
    probes = direction.shape[1]
    out = jax.ShapeDtypeStruct((probes, count), f32)
    dma = pltpu.SemaphoreType.DMA
    vmem = pltpu.VMEM
    outs = pl.pallas_call(
        step_kernel,
        out_shape=[out] * 3,
        in_specs=[pl.BlockSpec(memory_space=vmem)] * 6,
        out_specs=[pl.BlockSpec(memory_space=vmem)] * 3,
        scratch_shapes=[
            vmem((GROUP, PACK, count), bf16),
            vmem((HALF + 1, PACK, count), bf16),
            vmem((HALF + 1, count, 128), bf16),
            vmem((HALF + 1, count, 128), bf16),
            vmem((count, count), bf16),
            vmem((count, count), bf16),
            vmem((HALF + 1, probes, count), f32),
            vmem((GROUP, probes, count), f32),
            vmem((HALF + 1, probes, count), bf16),
            vmem((GROUP, probes, count), bf16),
            vmem((HALF + 1, probes, count), bf16),
            vmem((GROUP, probes, count), bf16),
            vmem((2, probes, 128), f32),
            vmem((GROUP, probes, 128), f32),
            vmem((GROUP, probes, 128), f32),
            dma((GROUP,)), dma((GROUP,)), dma((HALF + 1,)), dma((HALF + 1,)),
            dma((HALF + 1,)), dma((HALF + 1,)), dma((GROUP,)), dma((GROUP,)),
            dma((GROUP,)), dma((GROUP,)), dma((GROUP,)), dma((GROUP,)),
        ],
        compiler_params=pltpu.CompilerParams(
            collective_id=0, has_side_effects=True, vmem_limit_bytes=48 * 2**20),
        name="cg_step",
    )(points.T, lengthscale[None, :], weekday[None, :], solution.T, residual.T, direction.T)
    return tuple(v.T for v in outs)


def solution(mesh):
    split = P(("row", "col"), None)
    in_specs = (split, P(), P(("row", "col")), split, split, split)
    return jax.shard_map(
        per_device, mesh=mesh, in_specs=in_specs, out_specs=(split, split, split), check_vma=False
    )
```

time: 1020 us -> 133 us (0.13)
  blocking collectives: 337 us -> 0 us
  matrix products: 314 us -> 0 us
  local copies, waits for them, and re-layouts: 197 us -> 5.92 us
  waiting for transfers between devices: 143 us -> 0 us
  Pallas kernels: 0 us -> 125 us
  between operations: 14.9 us -> 0.66 us
    dot_general x81 -> x0, matrix products: 314 us -> none  [the longest x16 135 us: one_turn(): jnp.einsum('gpf,gqf->gpq', left_parts[0], right_parts[0], preferred_eleme...]
    gather x128 -> x0, local copies, waits for them, and re-layouts: 186 us -> none  [the longest x64 93 us: one_turn(): left_parts = [jnp.take(member, row_pick, axis=0) for member in row_blocks]]
    all_gather x6 -> x0, blocking collectives: 185 us -> none  [the longest x1 43.5 us: per_device(): lax.all_gather(scaled, 'col', axis=0, tiled=True)]
    psum x2 -> x0, blocking collectives: 152 us -> none  [the longest x1 79.2 us: per_device(): old_norm = lax.psum(jnp.sum(residual * residual, axis=0), ('row', 'col'))]
    reduce_scatter x2 -> x0, waiting for transfers between devices: 143 us -> none  [the longest x1 79.5 us: per_device(): lax.psum_scatter(row_partial, 'col', scatter_dimension=0, tiled=True)]
    pallas_call x0 -> x1, Pallas kernels: none -> 125 us  [per_device(): pl.pallas_call(step_kernel, out_shape=[out] * 3, in_specs=[pl.BlockSpec(m...]
  transfers between devices with their start and end apart: 2 -> 0, of which waited for: 2 -> 0; matrix products, arithmetic and copies ran while one was open for 0% -> 0% of each run, Pallas kernels for 0% -> 0%
where the time goes in v1:
time: 133 us; the launch traced here: 131 us
  Pallas kernels  125 us (94%)
  local copies, waits for them, and re-layouts  5.92 us (4%)
    pallas_call x1, Pallas kernels, per_device(): pl.pallas_call(step_kernel, out_shape=[out] * 3, in_specs=[pl.BlockSpec(m...  125 us
    unnamed x15, local copies, waits for them, and re-layouts  5.92 us

profile of v1, /device:TPU:1, one launch (start us, length us, event | category | flops | bytes accessed | tf_op | source)
XLA Modules:
  0.0 131.2 jit_solution(2171686779704646811)
XLA Ops:
  0.6 0.0 copy-start.4
  0.6 0.0 copy-start.5
  0.7 0.7 copy-done.4
  1.3 0.0 copy-done.5
  1.3 0.0 copy-start
  1.3 0.8 copy-done
  2.2 0.0 copy-start.1
  2.2 0.8 copy-done.1
  3.0 0.0 copy-start.2
  3.0 0.8 copy-done.2
  3.8 0.0 copy-start.3
  3.8 0.8 copy-done.3
  4.7 124.6 %cg_step.1 = (f32[32,512]{1,0:T(8,128)S(1)}, f32[32,512]{1,0:T(8,128)S(1)}, f32[32,512]{1,0:T(8,128)S(1)}) custom-call(f32[32,512]{1,0:T(8,128)S(1)} %bitcast.12, f32[1,32]{1,0:T(1,128)S(1)} %bitcast.17, s32[1,512]{1,0:T(1,128)S(1)} %bitcast.16, f32[32,512]{1,0:T(8,128)S(1)} %bitcast.13, f32[32,512]{1,0:T(8,128)S(1)} %bitcast.14, f32[32,512]{1,0:T(8,128)S(1)} %bitcast.15), custom_call_target="tpu_custom_call" | custom-call | tf_op jit(solution)/shard_map/cg_step/pallas_call | solution.py:289
  129.3 0.6 copy.12
  129.9 0.6 copy.13
  130.5 0.6 copy.14
Async XLA Ops:
  0.6 0.7 copy-start.4
  0.6 0.7 copy-start.5
  1.3 0.8 copy-start
  2.2 0.8 copy-start.1
  3.0 0.8 copy-start.2
  3.8 0.8 copy-start.3

commit v2 on v1

v2 whole, which is shorter than its diff:
```python
import functools

import jax
import jax.numpy as jnp
from jax import lax
from jax.experimental import pallas as pl
from jax.experimental.pallas import tpu as pltpu
from jax.sharding import PartitionSpec as P

f32 = jnp.float32
bf16 = jnp.bfloat16
MESH = pl.DeviceIdType.MESH

root_five = 2.23606797749979
log2_e = 1.4426950408889634
noise_level = 0.5
cross_day = 0.4

FEATS = 32
MISC = 64
SENT = 80
PACK = 112
DEPTH = PACK - FEATS
GROUP = 16
HALF = 8
STRETCH = 5.0 / 3.0 * log2_e
X_PER_ROOT = -(3.0 * log2_e) ** 0.5
OUT_SCALE = cross_day / log2_e
SAME_DAY = 1.0 / cross_day
LONG = 81
TILES = 129
TINY = 1e-30


def kernel_values(m, row_days, col_days):
    x = (m * lax.rsqrt(m)) * X_PER_ROOT
    e = jnp.exp2(x)
    k = (((m + log2_e) - x) * e).astype(bf16)
    return k * jnp.where(row_days == col_days, bf16(SAME_DAY), bf16(1.0))


def step_kernel(
    pts_any, ls_any, day_any, sol_any, res_any, dir_any,
    nsol_ref, nres_ref, ndir_ref,
    pts_ref, ls_ref, day_ref, sol_ref, res_ref, dir_ref, load,
    gcol, grow, xa, da, v0, v1, k0, k1, ro, co, rrow, rcol, stat, st1, st2,
    gc_send, gc_recv, fw_send, gr_send, gr_recv, rr_send, rr_recv, rc_send, rc_recv,
    s1_send, s1_recv, s2_send, s2_recv,
):
    r = lax.axis_index("row")
    c = lax.axis_index("col")

    def at_row(d):
        return (lax.rem(r + d, GROUP), c)

    def at_col(d):
        return (r, lax.rem(c + d + GROUP, GROUP))

    loads = [
        pltpu.make_async_copy(src, dst, load.at[n])
        for n, (src, dst) in enumerate((
            (ls_any, ls_ref), (pts_any, pts_ref), (day_any, day_ref),
            (dir_any, dir_ref), (res_any, res_ref), (sol_any, sol_ref)))
    ]
    for copy in loads:
        copy.start()

    barrier = pltpu.get_barrier_semaphore()

    def greet(d, _):
        pl.semaphore_signal(barrier, inc=1, device_id=at_row(d), device_id_type=MESH)
        pl.semaphore_signal(barrier, inc=1, device_id=at_col(d), device_id_type=MESH)
        return 0

    lax.fori_loop(1, GROUP, greet, 0)

    sent = pl.ds(0, SENT)

    def gather_col(d):
        return pltpu.make_async_remote_copy(
            src_ref=gcol.at[0, sent], dst_ref=gcol.at[d, sent], send_sem=gc_send,
            recv_sem=gc_recv.at[d], device_id=at_row(GROUP - d), device_id_type=MESH)

    side = 1 - 2 * lax.rem(r, 2)

    def forward(d):
        slot = lax.rem(d - side + GROUP, GROUP)
        return pltpu.make_async_remote_copy(
            src_ref=gcol.at[d, sent], dst_ref=gcol.at[slot, sent], send_sem=fw_send,
            recv_sem=gc_recv.at[slot], device_id=at_row(side + GROUP), device_id_type=MESH)

    def turn(d):
        return d * (2 * lax.rem(d, 2) - 1)

    def gather_row(d):
        return pltpu.make_async_remote_copy(
            src_ref=gcol.at[0, sent], dst_ref=grow.at[d], send_sem=gr_send,
            recv_sem=gr_recv.at[d], device_id=at_col(-turn(d)), device_id_type=MESH)

    def give_row(d):
        return pltpu.make_async_remote_copy(
            src_ref=ro.at[d], dst_ref=rrow.at[d], send_sem=rr_send,
            recv_sem=rr_recv, device_id=at_col(turn(d)), device_id_type=MESH)

    def give_col(d):
        return pltpu.make_async_remote_copy(
            src_ref=co.at[d], dst_ref=rcol.at[d], send_sem=rc_send,
            recv_sem=rc_recv, device_id=at_row(d), device_id_type=MESH)

    def share_row(d):
        return pltpu.make_async_remote_copy(
            src_ref=stat.at[0], dst_ref=st1.at[d], send_sem=s1_send,
            recv_sem=s1_recv, device_id=at_row(d), device_id_type=MESH)

    def share_col(d):
        return pltpu.make_async_remote_copy(
            src_ref=stat.at[1], dst_ref=st2.at[d], send_sem=s2_send,
            recv_sem=s2_recv, device_id=at_col(d), device_id_type=MESH)

    for copy in loads[:4]:
        copy.wait()
    direction = dir_ref[...]
    scales = jnp.transpose(jnp.broadcast_to(ls_ref[...], (128, 32)))[:, :1]
    scaled = (pts_ref[...] / scales).astype(bf16)
    wide = scaled.astype(f32)
    norm = jnp.sum(wide * wide, axis=0, keepdims=True) * STRETCH
    norm_hi = norm.astype(bf16).astype(f32)
    rest = norm - norm_hi
    norm_mid = rest.astype(bf16).astype(f32)
    norm_lo = rest - norm_mid
    points = norm.shape[1]
    line = lax.broadcasted_iota(jnp.int32, (16, points), 0)
    misc = jnp.where(line == 0, norm_hi, 0.0)
    misc = jnp.where(line == 1, norm_mid, misc)
    misc = jnp.where(line == 2, norm_lo, misc)
    misc = jnp.where((line >= 3) & (line < 6), 1.0, misc)
    misc = jnp.where(line == 6, day_ref[...].astype(f32), misc)
    for own in (gcol, grow):
        own[0, :FEATS, :] = direction.astype(bf16)
        own[0, FEATS:MISC, :] = scaled
        own[0, MISC:SENT, :] = misc.astype(bf16)
    gcol[0, SENT:, :] = scaled

    ro[...] = jnp.zeros_like(ro)
    co[...] = jnp.zeros_like(co)

    def prepare(i):
        extra = grow[i, MISC:SENT, :].astype(f32)
        ones = jnp.where(line < 3, 1.0, jnp.where(line < 6, pltpu.roll(extra, 3, 0), 0.0))
        left = grow[i, FEATS:MISC, :].astype(f32) * (-2.0 * STRETCH)
        high = left.astype(bf16).astype(f32)
        block = jnp.concatenate(
            [high, ones, left - high, jnp.zeros((128 - DEPTH, points), f32)], axis=0)
        xa[i] = jnp.transpose(block).astype(bf16)
        da[i] = jnp.transpose(jnp.broadcast_to(extra[6:7, :], (128, points))).astype(bf16)

    rows = points // 2
    halves = (slice(0, rows), slice(rows, points))

    def distances(v, i, j, h):
        squared = jnp.dot(xa[i, halves[h], :DEPTH], gcol[j, FEATS:, :], preferred_element_type=f32)
        v[...] = jnp.maximum(squared, TINY)

    def values(v, k, i, j, h):
        days = jnp.concatenate([da[i, halves[h], :]] * (points // 128), axis=1)
        k[...] = kernel_values(v[...], days, gcol[j, MISC + 6:MISC + 7, :])

    def apply(k, i, j, h, kept=None):
        row_part = lax.dot_general(
            gcol[j, :FEATS, :], k[...], (((1,), (1,)), ((), ())), preferred_element_type=f32)
        col_part = jnp.dot(grow[i, :FEATS, halves[h]], k[...], preferred_element_type=f32)
        if kept is not None:
            row_part, col_part = row_part * kept, col_part * kept
        ro[i, :, halves[h]] += row_part
        co[j] += col_part

    def where_is(t):
        p = lax.rem(t + HALF, GROUP)
        q = lax.rem(p, HALF)
        line = lax.div(t + HALF, GROUP)
        turned = t - LONG
        return (
            jnp.where(t < HALF, 0, jnp.where(t < LONG, 3 + line, 1 + lax.div(lax.rem(turned, 12), 4))),
            jnp.where(t < LONG, p - q + lax.rem(2 * q, HALF) + lax.div(q, 4),
                      lax.rem(4 * lax.div(turned, 12) + lax.rem(turned, 4) + 1, GROUP)))

    prepare(0)
    for h in range(2):
        distances(v0, 0, 0, h)
        values(v0, k0, 0, 0, h)
        co[0] += jnp.dot(grow[0, :FEATS, halves[h]], k0[...], preferred_element_type=f32)
    k1[...] = jnp.zeros_like(k1)

    pl.semaphore_wait(barrier, 2 * (GROUP - 1))

    def send_col(n, _):
        gather_col(2 * n).start()
        return 0

    forward(0).start()
    lax.fori_loop(HALF // 2, HALF, send_col, 0)
    gather_row(4).start()
    lax.fori_loop(1, HALF // 2, send_col, 0)

    row_kept = jnp.where(r < HALF, 1.0, 0.0)
    col_kept = jnp.where(c < HALF, 1.0, 0.0)

    def arrived(j):
        gather_col(j).wait_recv()
        gcol[j, SENT:, :] = gcol[j, FEATS:MISC, :]

        @pl.when(lax.rem(j, 2) == 0)
        def _():
            forward(j).start()

    arrived(HALF)
    distances(v0, 0, HALF, 0)

    def two(m, places):
        t = 2 * m
        i_, j_, i0, j0 = places
        i1, j1 = where_is(t + 1)
        i2, j2 = where_is(t + 2)

        @pl.when(t < LONG)
        def _():
            @pl.when(t < GROUP)
            def _():
                arrived(j1)

                @pl.when((t != HALF - 2) & (t != GROUP - 2))
                def _():
                    arrived(j2)

            @pl.when(lax.rem(t, GROUP) == HALF - 2)
            def _():
                gather_row(i2).wait_recv()

                @pl.when(i2 < HALF)
                def _():
                    gather_row(i2 + 1).start()

                @pl.when(i2 == HALF - 1)
                def _():
                    for n in (1, 2, 3):
                        gather_row(n).start()

                @pl.when(i2 > 5)
                def _():
                    give_row(i2 - 2).start()

                prepare(i2)

            @pl.when(t == LONG - 1)
            def _():
                def ready(n, _):
                    gather_row(n).wait_recv()
                    prepare(n)
                    return 0

                lax.fori_loop(1, 4, ready, 0)
                give_row(7).start()

        kept = jnp.where((t == 0) | (t == LONG - 1), row_kept, jnp.where(t == LONG - 9, col_kept, 1.0))
        apply(k1, i_, j_, 1)
        distances(v1, i0, j0, 1)
        values(v0, k0, i0, j0, 0)
        apply(k0, i0, j0, 0, kept)
        distances(v0, i1, j1, 0)
        values(v1, k1, i0, j0, 1)
        apply(k1, i0, j0, 1, kept)
        distances(v1, i1, j1, 1)
        values(v0, k0, i1, j1, 0)
        apply(k0, i1, j1, 0)
        distances(v0, i2, j2, 0)
        values(v1, k1, i1, j1, 1)

        @pl.when(t >= LONG - 1)
        def _():
            @pl.when((i_ == 3) & (j_ != 0))
            def _():
                give_col(j_).start()

            @pl.when((i0 == 3) & (j0 != 0))
            def _():
                give_col(j0).start()

            for n, done in ((8, LONG - 1), (1, TILES - 9), (2, TILES - 5)):
                @pl.when(t == done)
                def _(n=n):
                    give_row(n).start()

        return i1, j1, i2, j2

    begin = jnp.int32(0)
    lax.fori_loop(0, TILES // 2, two, (begin, begin, begin, begin + HALF))
    apply(k1, 3, GROUP - 1, 1)
    distances(v1, 3, 0, 1)
    values(v0, k0, 3, 0, 0)
    give_col(GROUP - 1).start()
    apply(k0, 3, 0, 0)
    values(v1, k1, 3, 0, 1)
    apply(k1, 3, 0, 1)
    give_row(3).start()

    def all_of(ref, count, sem):
        part = ref.at[pl.ds(1, count)]
        pltpu.make_async_copy(part, part, sem).wait()

    all_of(rcol, GROUP - 1, rc_recv)
    all_of(rrow, HALF, rr_recv)
    applied = ro[0] + co[0]
    for n in range(1, GROUP):
        applied = applied + rcol[n]
    for n in range(1, HALF + 1):
        applied = applied + rrow[n]

    image = applied * OUT_SCALE + noise_level * direction
    for copy in loads[4:]:
        copy.wait()
    residual = res_ref[...]
    lane = lax.broadcasted_iota(jnp.int32, (32, 128), 1)
    blank = jnp.zeros((96, 128), f32)
    sums = [residual * residual, direction * image, residual * image, image * image]
    sums = [jnp.sum(v, axis=1, keepdims=True) for v in sums]
    packed = jnp.where(lane == 0, sums[0], jnp.where(lane == 1, sums[1], jnp.where(lane == 2, sums[2], sums[3])))

    def exchange(slot, packed, copy, landing, sem):
        stat[slot] = packed

        def begin(d, _):
            copy(d).start()
            return 0

        lax.fori_loop(1, GROUP, begin, 0)
        all_of(landing, GROUP - 1, sem)
        for n in range(1, GROUP):
            packed = packed + landing[n]
        return packed

    packed = jnp.transpose(jnp.concatenate([packed, blank], axis=0))[:8]
    packed = exchange(0, packed, share_row, st1, s1_recv)
    packed = exchange(1, packed, share_col, st2, s2_recv)
    packed = jnp.transpose(jnp.concatenate([packed, blank, blank[:24]], axis=0))[:32]
    old_norm, curvature, mixed, image_norm = (packed[:, n:n + 1] for n in range(4))
    step = old_norm / curvature
    new_norm = old_norm - 2.0 * step * mixed + step * step * image_norm
    new_residual = residual - step * image
    nsol_ref[...] = sol_ref[...] + step * direction
    nres_ref[...] = new_residual
    ndir_ref[...] = new_residual + new_norm / old_norm * direction

    def all_sent(ref, count, sem):
        part = ref.at[pl.ds(0, count)]
        pltpu.make_async_copy(part, part, sem).wait()

    all_sent(grow, HALF - 1, gc_send)
    all_sent(grow, HALF, gr_send)
    all_sent(grow, HALF, fw_send)
    all_sent(co, GROUP - 1, rc_send)
    all_sent(ro, HALF, rr_send)
    all_sent(st1, GROUP - 1, s1_send)
    all_sent(st2, GROUP - 1, s2_send)


def per_device(points, lengthscale, weekday, solution, residual, direction):
    count, feats = points.shape
    probes = direction.shape[1]
    out = jax.ShapeDtypeStruct((probes, count), f32)
    dma = pltpu.SemaphoreType.DMA
    vmem = pltpu.VMEM
    outs = pl.pallas_call(
        step_kernel,
        out_shape=[out] * 3,
        in_specs=[pl.BlockSpec(memory_space=pl.ANY)] * 6,
        out_specs=[pl.BlockSpec(memory_space=vmem)] * 3,
        scratch_shapes=[
            vmem((feats, count), f32), vmem((1, feats), f32), vmem((1, count), jnp.int32),
            vmem((probes, count), f32), vmem((probes, count), f32), vmem((probes, count), f32),
            dma((6,)),
            vmem((GROUP, PACK, count), bf16),
            vmem((HALF + 1, SENT, count), bf16),
            vmem((HALF + 1, count, 128), bf16),
            vmem((HALF + 1, count, 128), bf16),
            vmem((count // 2, count), f32),
            vmem((count // 2, count), f32),
            vmem((count // 2, count), bf16),
            vmem((count // 2, count), bf16),
            vmem((HALF + 1, probes, count), f32),
            vmem((GROUP, probes, count), f32),
            vmem((HALF + 1, probes, count), f32),
            vmem((GROUP, probes, count), f32),
            vmem((2, 8, 128), f32),
            vmem((GROUP, 8, 128), f32),
            vmem((GROUP, 8, 128), f32),
            dma, dma((GROUP,)), dma, dma, dma((HALF + 1,)),
            dma, dma, dma, dma, dma, dma, dma, dma,
        ],
        compiler_params=pltpu.CompilerParams(
            collective_id=0, has_side_effects=True, vmem_limit_bytes=48 * 2**20),
        name="cg_step",
    )(points.T, lengthscale[None, :], weekday[None, :], solution.T, residual.T, direction.T)
    return tuple(v.T for v in outs)


def solution(mesh):
    split = P(("row", "col"), None)
    in_specs = (split, P(), P(("row", "col")), split, split, split)
    return jax.shard_map(
        per_device, mesh=mesh, in_specs=in_specs, out_specs=(split, split, split), check_vma=False
    )
```

time: 133 us -> 110 us (0.83); the launches traced: 131 us -> 110 us
  Pallas kernels: 125 us -> 104 us
    pallas_call x1, Pallas kernels: 125 us -> 104 us  [per_device(): pl.pallas_call(step_kernel, out_shape=[out] * 3, in_specs=[pl.BlockSpec(m...]
where the time goes in v2:
time: 110 us
  Pallas kernels  104 us (95%)
  local copies, waits for them, and re-layouts  5.92 us (5%)
    pallas_call x1, Pallas kernels, per_device(): pl.pallas_call(step_kernel, out_shape=[out] * 3, in_specs=[pl.BlockSpec(m...  104 us
    unnamed x15, local copies, waits for them, and re-layouts  5.92 us

profile of v2, /device:TPU:1, one launch (start us, length us, event | category | flops | bytes accessed | tf_op | source)
XLA Modules:
  0.0 110.2 jit_solution(15478317786277669625)
XLA Ops:
  0.6 0.0 copy-start.4
  0.6 0.0 copy-start.5
  0.7 0.7 copy-done.4
  1.3 0.0 copy-done.5
  1.3 0.0 copy-start
  1.3 0.8 copy-done
  2.2 0.0 copy-start.1
  2.2 0.8 copy-done.1
  3.0 0.0 copy-start.2
  3.0 0.8 copy-done.2
  3.8 0.0 copy-start.3
  3.8 0.8 copy-done.3
  4.7 103.6 %cg_step.1 = (f32[32,512]{1,0:T(8,128)S(1)}, f32[32,512]{1,0:T(8,128)S(1)}, f32[32,512]{1,0:T(8,128)S(1)}) custom-call(f32[32,512]{1,0:T(8,128)S(1)} %bitcast.12, f32[1,32]{1,0:T(1,128)S(1)} %bitcast.17, s32[1,512]{1,0:T(1,128)S(1)} %bitcast.16, f32[32,512]{1,0:T(8,128)S(1)} %bitcast.13, f32[32,512]{1,0:T(8,128)S(1)} %bitcast.14, f32[32,512]{1,0:T(8,128)S(1)} %bitcast.15), custom_call_target="tpu_custom_call" | custom-call | tf_op jit(solution)/shard_map/cg_step/pallas_call | solution.py:372
  108.3 0.6 copy.12
  108.9 0.6 copy.13
  109.6 0.6 copy.14
Async XLA Ops:
  0.6 0.7 copy-start.4
  0.6 0.7 copy-start.5
  1.3 0.8 copy-start
  2.2 0.8 copy-start.1
  3.0 0.8 copy-start.2
  3.8 0.8 copy-start.3

commit v3 on v2

--- a/solution.py
+++ b/solution.py
@@ -27,8 +27,11 @@
 X_PER_ROOT = -(3.0 * log2_e) ** 0.5
 OUT_SCALE = cross_day / log2_e
 SAME_DAY = 1.0 / cross_day
+AWAY = HALF + 1
+FAR = 1e6
 LONG = 81
 TILES = 129
+LATE = 13
 TINY = 1e-30
 
 
@@ -40,12 +43,12 @@
 
 
 def step_kernel(
-    pts_any, ls_any, day_any, sol_any, res_any, dir_any,
-    nsol_ref, nres_ref, ndir_ref,
-    pts_ref, ls_ref, day_ref, sol_ref, res_ref, dir_ref, load,
-    gcol, grow, xa, da, v0, v1, k0, k1, ro, co, rrow, rcol, stat, st1, st2,
+    pts_any, ls_any, day_any, res_any, dir_any,
+    image_ref, factors_ref,
+    pts_ref, ls_ref, day_ref, res_ref, dir_ref, load,
+    gcol, grow, xa, da, v0, v1, k0, k1, ro, co, rrow, rcol, late, landed, stat, st1, st2,
     gc_send, gc_recv, fw_send, gr_send, gr_recv, rr_send, rr_recv, rc_send, rc_recv,
-    s1_send, s1_recv, s2_send, s2_recv,
+    s1_send, s1_recv, s2_send, s2_recv, late_send, late_recv,
 ):
     r = lax.axis_index("row")
     c = lax.axis_index("col")
@@ -60,7 +63,7 @@
         pltpu.make_async_copy(src, dst, load.at[n])
         for n, (src, dst) in enumerate((
             (ls_any, ls_ref), (pts_any, pts_ref), (day_any, day_ref),
-            (dir_any, dir_ref), (res_any, res_ref), (sol_any, sol_ref)))
+            (dir_any, dir_ref), (res_any, res_ref)))
     ]
     for copy in loads:
         copy.start()
@@ -106,6 +109,18 @@
         return pltpu.make_async_remote_copy(
             src_ref=co.at[d], dst_ref=rcol.at[d], send_sem=rc_send,
             recv_sem=rc_recv, device_id=at_row(d), device_id_type=MESH)
+
+    def give_late(n, ref, d, place):
+        late[n] = ref[d].astype(bf16)
+        pltpu.make_async_remote_copy(
+            src_ref=late.at[n], dst_ref=landed.at[n], send_sem=late_send,
+            recv_sem=late_recv, device_id=place, device_id_type=MESH).start()
+
+    def late_row(d):
+        give_late(d - 1, ro, d, at_col(turn(d)))
+
+    def late_col(d):
+        give_late(d - LATE + 3, co, d, at_row(d))
 
     def share_row(d):
         return pltpu.make_async_remote_copy(
@@ -165,24 +180,27 @@
         days = jnp.concatenate([da[i, halves[h], :]] * (points // 128), axis=1)
         k[...] = kernel_values(v[...], days, gcol[j, MISC + 6:MISC + 7, :])
 
-    def apply(k, i, j, h, kept=None):
+    def apply(k, i, j, h):
         row_part = lax.dot_general(
             gcol[j, :FEATS, :], k[...], (((1,), (1,)), ((), ())), preferred_element_type=f32)
         col_part = jnp.dot(grow[i, :FEATS, halves[h]], k[...], preferred_element_type=f32)
-        if kept is not None:
-            row_part, col_part = row_part * kept, col_part * kept
         ro[i, :, halves[h]] += row_part
         co[j] += col_part
 
-    def where_is(t):
+    def early_place(t):
         p = lax.rem(t + HALF, GROUP)
         q = lax.rem(p, HALF)
         line = lax.div(t + HALF, GROUP)
-        turned = t - LONG
+        shift = jnp.where(t < HALF, 4, 0)
         return (
-            jnp.where(t < HALF, 0, jnp.where(t < LONG, 3 + line, 1 + lax.div(lax.rem(turned, 12), 4))),
-            jnp.where(t < LONG, p - q + lax.rem(2 * q, HALF) + lax.div(q, 4),
-                      lax.rem(4 * lax.div(turned, 12) + lax.rem(turned, 4) + 1, GROUP)))
+            jnp.where(t < HALF, 0, 3 + line),
+            p - q + lax.rem(2 * q + shift, HALF) + lax.div(q, 4))
+
+    def late_place(t):
+        turned = lax.rem(t - LONG, 12)
+        return (
+            1 + lax.div(turned, 4),
+            lax.rem(4 * lax.div(t - LONG, 12) + lax.rem(turned, 4) + 1, GROUP))
 
     prepare(0)
     for h in range(2):
@@ -190,6 +208,8 @@
         values(v0, k0, 0, 0, h)
         co[0] += jnp.dot(grow[0, :FEATS, halves[h]], k0[...], preferred_element_type=f32)
     k1[...] = jnp.zeros_like(k1)
+    lane = lax.broadcasted_iota(jnp.int32, (points, 128), 1)
+    xa[AWAY] = jnp.where(lane == MISC - FEATS + 3, FAR, 0.0).astype(bf16)
 
     pl.semaphore_wait(barrier, 2 * (GROUP - 1))
 
@@ -198,12 +218,15 @@
         return 0
 
     forward(0).start()
-    lax.fori_loop(HALF // 2, HALF, send_col, 0)
+    for n in (6, 7, 4, 5):
+        send_col(n, 0)
     gather_row(4).start()
     lax.fori_loop(1, HALF // 2, send_col, 0)
 
-    row_kept = jnp.where(r < HALF, 1.0, 0.0)
-    col_kept = jnp.where(c < HALF, 1.0, 0.0)
+    def left_of(t, i):
+        along_row = (t == 2) | (t == LONG - 1)
+        gone = (along_row & (r >= HALF)) | ((t == LONG - 9) & (c >= HALF))
+        return jnp.where(gone, AWAY, i)
 
     def arrived(j):
         gather_col(j).wait_recv()
@@ -213,107 +236,116 @@
         def _():
             forward(j).start()
 
-    arrived(HALF)
-    distances(v0, 0, HALF, 0)
-
-    def two(m, places):
+    arrived(HALF + 4)
+    distances(v0, 0, HALF + 4, 0)
+
+    def early(m, places):
         t = 2 * m
-        i_, j_, i0, j0 = places
-        i1, j1 = where_is(t + 1)
-        i2, j2 = where_is(t + 2)
-
-        @pl.when(t < LONG)
+        tile1 = i1, j1 = early_place(t + 1)
+        i2, j2 = early_place(t + 2)
+
+        @pl.when(t < GROUP)
         def _():
-            @pl.when(t < GROUP)
+            arrived(j1)
+
+            @pl.when((t != HALF - 2) & (t != GROUP - 2))
             def _():
-                arrived(j1)
-
-                @pl.when((t != HALF - 2) & (t != GROUP - 2))
-                def _():
-                    arrived(j2)
-
-            @pl.when(lax.rem(t, GROUP) == HALF - 2)
+                arrived(j2)
+
+        @pl.when(lax.rem(t, GROUP) == HALF - 2)
+        def _():
+            gather_row(i2).wait_recv()
+
+            @pl.when(i2 < HALF)
             def _():
-                gather_row(i2).wait_recv()
-
-                @pl.when(i2 < HALF)
-                def _():
-                    gather_row(i2 + 1).start()
-
-                @pl.when(i2 == HALF - 1)
-                def _():
-                    for n in (1, 2, 3):
-                        gather_row(n).start()
-
-                @pl.when(i2 > 5)
-                def _():
-                    give_row(i2 - 2).start()
-
-                prepare(i2)
-
-            @pl.when(t == LONG - 1)
+                gather_row(i2 + 1).start()
+
+            @pl.when(i2 == HALF - 1)
             def _():
-                def ready(n, _):
-                    gather_row(n).wait_recv()
-                    prepare(n)
-                    return 0
-
-                lax.fori_loop(1, 4, ready, 0)
-                give_row(7).start()
-
-        kept = jnp.where((t == 0) | (t == LONG - 1), row_kept, jnp.where(t == LONG - 9, col_kept, 1.0))
+                for n in (1, 2, 3):
+                    gather_row(n).start()
+
+            @pl.when(i2 > 5)
+            def _():
+                give_row(i2 - 2).start()
+
+            prepare(i2)
+
+        left2 = left_of(t + 2, i2)
+        two_tiles(places, tile1, (left2, i2, j2))
+        return i1, j1, left2, i2, j2
+
+    def two_tiles(places, tile1, tile2):
+        i_, j_, left0, i0, j0 = places
+        i1, j1 = tile1
+        left2, i2, j2 = tile2
+
         apply(k1, i_, j_, 1)
-        distances(v1, i0, j0, 1)
+        distances(v1, left0, j0, 1)
         values(v0, k0, i0, j0, 0)
-        apply(k0, i0, j0, 0, kept)
+        apply(k0, i0, j0, 0)
         distances(v0, i1, j1, 0)
         values(v1, k1, i0, j0, 1)
-        apply(k1, i0, j0, 1, kept)
+        apply(k1, i0, j0, 1)
         distances(v1, i1, j1, 1)
         values(v0, k0, i1, j1, 0)
         apply(k0, i1, j1, 0)
-        distances(v0, i2, j2, 0)
+        distances(v0, left2, j2, 0)
         values(v1, k1, i1, j1, 1)
 
-        @pl.when(t >= LONG - 1)
-        def _():
-            @pl.when((i_ == 3) & (j_ != 0))
-            def _():
-                give_col(j_).start()
-
-            @pl.when((i0 == 3) & (j0 != 0))
-            def _():
-                give_col(j0).start()
-
-            for n, done in ((8, LONG - 1), (1, TILES - 9), (2, TILES - 5)):
-                @pl.when(t == done)
-                def _(n=n):
-                    give_row(n).start()
-
-        return i1, j1, i2, j2
+    def late_tiles(m, places):
+        t = 2 * m
+        i_, j_, _, i0, j0 = places
+        tile1 = i1, j1 = late_place(t + 1)
+        i2, j2 = late_place(t + 2)
+        two_tiles(places, tile1, (i2, i2, j2))
+
+        for i, j in ((i_, j_), (i0, j0)):
+            @pl.when((i == 3) & (j < LATE))
+            def _(j=j):
+                give_col(j).start()
+
+        for done, send in (
+            (LONG - 1, lambda: give_row(8).start()),
+            (TILES - 9, lambda: late_row(1)),
+            (TILES - 5, lambda: late_row(2)),
+            (TILES - 3, lambda: (late_col(LATE), late_col(LATE + 1))),
+        ):
+            pl.when(t == done)(lambda send=send: (send(), None)[1])
+
+        return i1, j1, i2, i2, j2
 
     begin = jnp.int32(0)
-    lax.fori_loop(0, TILES // 2, two, (begin, begin, begin, begin + HALF))
+    places = (begin, begin, begin, begin, begin + HALF + 4)
+    places = lax.fori_loop(0, LONG // 2, early, places)
+    for n in (1, 2, 3):
+        gather_row(n).wait_recv()
+        prepare(n)
+    give_row(7).start()
+    lax.fori_loop(LONG // 2, TILES // 2, late_tiles, places)
     apply(k1, 3, GROUP - 1, 1)
     distances(v1, 3, 0, 1)
     values(v0, k0, 3, 0, 0)
-    give_col(GROUP - 1).start()
+    late_col(GROUP - 1)
     apply(k0, 3, 0, 0)
     values(v1, k1, 3, 0, 1)
     apply(k1, 3, 0, 1)
-    give_row(3).start()
-
-    def all_of(ref, count, sem):
-        part = ref.at[pl.ds(1, count)]
+    late_row(3)
+
+    def all_of(ref, start, count, sem):
+        part = ref.at[pl.ds(start, count)]
         pltpu.make_async_copy(part, part, sem).wait()
 
-    all_of(rcol, GROUP - 1, rc_recv)
-    all_of(rrow, HALF, rr_recv)
+    all_of(rcol, 1, LATE - 1, rc_recv)
+    all_of(rrow, 4, HALF - 3, rr_recv)
     applied = ro[0] + co[0]
-    for n in range(1, GROUP):
+    for n in range(1, LATE):
         applied = applied + rcol[n]
-    for n in range(1, HALF + 1):
+    for n in range(4, HALF + 1):
         applied = applied + rrow[n]
+    all_of(landed, 0, 6, late_recv)
+    for n in range(6):
+        applied = applied + landed[n].astype(f32)
 
     image = applied * OUT_SCALE + noise_level * direction
     for copy in loads[4:]:
@@ -333,7 +365,7 @@
             return 0
 
         lax.fori_loop(1, GROUP, begin, 0)
-        all_of(landing, GROUP - 1, sem)
+        all_of(landing, 1, GROUP - 1, sem)
         for n in range(1, GROUP):
             packed = packed + landing[n]
         return packed
@@ -345,22 +377,18 @@
     old_norm, curvature, mixed, image_norm = (packed[:, n:n + 1] for n in range(4))
     step = old_norm / curvature
     new_norm = old_norm - 2.0 * step * mixed + step * step * image_norm
-    new_residual = residual - step * image
-    nsol_ref[...] = sol_ref[...] + step * direction
-    nres_ref[...] = new_residual
-    ndir_ref[...] = new_residual + new_norm / old_norm * direction
-
-    def all_sent(ref, count, sem):
-        part = ref.at[pl.ds(0, count)]
-        pltpu.make_async_copy(part, part, sem).wait()
-
-    all_sent(grow, HALF - 1, gc_send)
-    all_sent(grow, HALF, gr_send)
-    all_sent(grow, HALF, fw_send)
-    all_sent(co, GROUP - 1, rc_send)
-    all_sent(ro, HALF, rr_send)
-    all_sent(st1, GROUP - 1, s1_send)
-    all_sent(st2, GROUP - 1, s2_send)
+    lane = lax.broadcasted_iota(jnp.int32, (32, 128), 1)
+    image_ref[...] = image
+    factors_ref[...] = jnp.where(lane == 0, step, new_norm / old_norm)
+
+    all_of(grow, 0, HALF - 1, gc_send)
+    all_of(grow, 0, HALF, gr_send)
+    all_of(grow, 0, HALF, fw_send)
+    all_of(co, 0, LATE - 1, rc_send)
+    all_of(ro, 0, HALF - 3, rr_send)
+    all_of(late, 0, 6, late_send)
+    all_of(st1, 0, GROUP - 1, s1_send)
+    all_of(st2, 0, GROUP - 1, s2_send)
 
 
 def per_device(points, lengthscale, weekday, solution, residual, direction):
@@ -369,18 +397,18 @@
     out = jax.ShapeDtypeStruct((probes, count), f32)
     dma = pltpu.SemaphoreType.DMA
     vmem = pltpu.VMEM
-    outs = pl.pallas_call(
+    image, factors = pl.pallas_call(
         step_kernel,
-        out_shape=[out] * 3,
-        in_specs=[pl.BlockSpec(memory_space=pl.ANY)] * 6,
-        out_specs=[pl.BlockSpec(memory_space=vmem)] * 3,
+        out_shape=[out, jax.ShapeDtypeStruct((probes, 128), f32)],
+        in_specs=[pl.BlockSpec(memory_space=pl.ANY)] * 5,
+        out_specs=[pl.BlockSpec(memory_space=vmem)] * 2,
         scratch_shapes=[
             vmem((feats, count), f32), vmem((1, feats), f32), vmem((1, count), jnp.int32),
-            vmem((probes, count), f32), vmem((probes, count), f32), vmem((probes, count), f32),
-            dma((6,)),
+            vmem((probes, count), f32), vmem((probes, count), f32),
+            dma((5,)),
             vmem((GROUP, PACK, count), bf16),
             vmem((HALF + 1, SENT, count), bf16),
-            vmem((HALF + 1, count, 128), bf16),
+            vmem((AWAY + 1, count, 128), bf16),
             vmem((HALF + 1, count, 128), bf16),
             vmem((count // 2, count), f32),
             vmem((count // 2, count), f32),
@@ -390,17 +418,23 @@
             vmem((GROUP, probes, count), f32),
             vmem((HALF + 1, probes, count), f32),
             vmem((GROUP, probes, count), f32),
+            vmem((6, probes, count), bf16),
+            vmem((6, probes, count), bf16),
             vmem((2, 8, 128), f32),
             vmem((GROUP, 8, 128), f32),
             vmem((GROUP, 8, 128), f32),
             dma, dma((GROUP,)), dma, dma, dma((HALF + 1,)),
-            dma, dma, dma, dma, dma, dma, dma, dma,
+            dma, dma, dma, dma, dma, dma, dma, dma, dma, dma,
         ],
         compiler_params=pltpu.CompilerParams(
             collective_id=0, has_side_effects=True, vmem_limit_bytes=48 * 2**20),
         name="cg_step",
-    )(points.T, lengthscale[None, :], weekday[None, :], solution.T, residual.T, direction.T)
-    return tuple(v.T for v in outs)
+    )(points.T, lengthscale[None, :], weekday[None, :], residual.T, direction.T)
+    step, ratio = factors[:, 0:1], factors[:, 1:2]
+    new_residual = residual.T - step * image
+    new_solution = solution.T + step * direction.T
+    new_direction = new_residual + ratio * direction.T
+    return new_solution.T, new_residual.T, new_direction.T
 
 
 def solution(mesh):

time: 110 us -> 106 us (0.964)
  Pallas kernels: 104 us -> 99.6 us
  local copies, waits for them, and re-layouts: 5.92 us -> 3.47 us
  other arithmetic: 0 us -> 1.43 us
    pallas_call x1, Pallas kernels: 104 us -> 99.6 us  [per_device(): pl.pallas_call(step_kernel, out_shape=[out, jax.ShapeDtypeStruct((probes,...]
    unnamed x15 -> x12, local copies, waits for them, and re-layouts: 5.92 us -> 3.3 us
where the time goes in v3:
time: 106 us; the launch traced here: 105 us
  Pallas kernels  99.6 us (94%)
  local copies, waits for them, and re-layouts  3.47 us (3%)
  other arithmetic  1.43 us (1%)
    pallas_call x1, Pallas kernels, per_device(): pl.pallas_call(step_kernel, out_shape=[out, jax.ShapeDtypeStruct((probes,...  99.6 us
    unnamed x12, local copies, waits for them, and re-layouts  3.3 us

profile of v3, /device:TPU:1, one launch (start us, length us, event | category | flops | bytes accessed | tf_op | source)
XLA Modules:
  0.0 105.2 jit_solution(7547717596836454980)
XLA Ops:
  0.6 0.0 copy-start.3
  0.6 0.0 copy-start.4
  0.7 0.7 copy-done.3
  1.3 0.0 copy-done.4
  1.3 0.0 copy-start
  1.3 0.8 copy-done
  2.2 0.0 copy-start.1
  2.2 0.8 copy-done.1
  3.0 0.0 copy-start.2
  3.0 0.8 copy-done.2
  3.8 99.6 %cg_step.1 = (f32[32,512]{1,0:T(8,128)S(1)}, f32[32,128]{1,0:T(8,128)S(1)}) custom-call(f32[32,512]{1,0:T(8,128)S(1)} %bitcast.14, f32[1,32]{1,0:T(1,128)S(1)} %bitcast.16, s32[1,512]{1,0:T(1,128)S(1)} %bitcast.15, f32[32,512]{1,0:T(8,128)S(1)} %bitcast.13, f32[32,512]{1,0:T(8,128)S(1)} %bitcast.12), custom_call_target="tpu_custom_call" | custom-call | tf_op jit(solution)/shard_map/cg_step/pallas_call | solution.py:400
  103.5 0.2 slice_reduce_fusion
  103.7 0.0 copy-start.5
  103.7 0.7 add_bitcast_fusion
  104.4 0.1 copy-done.5
  104.5 0.7 multiply_add_fusion
Async XLA Ops:
  0.6 0.7 copy-start.3
  0.6 0.7 copy-start.4
  1.3 0.8 copy-start
  2.2 0.8 copy-start.1
  3.0 0.8 copy-start.2
  103.7 0.8 copy-start.5

commit v4 on v3

--- a/solution.py
+++ b/solution.py
@@ -36,9 +36,9 @@
 
 
 def kernel_values(m, row_days, col_days):
-    x = (m * lax.rsqrt(m)) * X_PER_ROOT
-    e = jnp.exp2(x)
-    k = (((m + log2_e) - x) * e).astype(bf16)
+    x = (m * X_PER_ROOT) * lax.rsqrt(m)
+    p = m - (x - log2_e)
+    k = (jnp.exp2(x) * p).astype(bf16)
     return k * jnp.where(row_days == col_days, bf16(SAME_DAY), bf16(1.0))
 
 
@@ -427,7 +427,7 @@
             dma, dma, dma, dma, dma, dma, dma, dma, dma, dma,
         ],
         compiler_params=pltpu.CompilerParams(
-            collective_id=0, has_side_effects=True, vmem_limit_bytes=48 * 2**20),
+            collective_id=0, has_side_effects=True, vmem_limit_bytes=62 * 2**20),
         name="cg_step",
     )(points.T, lengthscale[None, :], weekday[None, :], residual.T, direction.T)
     step, ratio = factors[:, 0:1], factors[:, 1:2]

time: 106 us -> 105 us (level)
  local copies, waits for them, and re-layouts: 3.47 us -> 0.99 us
  Pallas kernels: 99.6 us -> 101 us
    unnamed x12 -> x6, local copies, waits for them, and re-layouts: 3.3 us -> 0.01 us
    pallas_call x1, Pallas kernels: 99.6 us -> 101 us  [per_device(): pl.pallas_call(step_kernel, out_shape=[out, jax.ShapeDtypeStruct((probes,...]
where the time goes in v4:
time: 105 us
  Pallas kernels  101 us (96%)
  other arithmetic  2.3 us (2%)
    pallas_call x1, Pallas kernels, per_device(): pl.pallas_call(step_kernel, out_shape=[out, jax.ShapeDtypeStruct((probes,...  101 us

profile of v4, /device:TPU:1, one launch (start us, length us, event | category | flops | bytes accessed | tf_op | source)
XLA Modules:
  0.0 104.7 jit_solution(4324617647433132834)
XLA Ops:
  0.6 0.0 copy-start
  0.6 0.0 copy-start.1
  0.7 100.7 %cg_step.1 = (f32[32,512]{1,0:T(8,128)}, f32[32,128]{1,0:T(8,128)}) custom-call(f32[32,512]{1,0:T(8,128)} %bitcast.14, f32[1,32]{1,0:T(1,128)} %bitcast.16, s32[1,512]{1,0:T(1,128)} %bitcast.15, f32[32,512]{1,0:T(8,128)} %bitcast.13, f32[32,512]{1,0:T(8,128)} %bitcast.12), custom_call_target="tpu_custom_call" | custom-call | tf_op jit(solution)/shard_map/cg_step/pallas_call | solution.py:400
  101.4 1.0 slice_reduce_fusion
  102.4 0.0 copy-done
  102.4 0.0 copy-done.1
  102.4 0.0 copy-start.2
  102.4 1.6 %add_bitcast_fusion = (f32[512,32]{0,1:T(8,128)}, f32[512,32]{0,1:T(8,128)}) fusion(f32[32]{0:T(128)S(1)} %get-tuple-element.7, f32[32,512]{1,0:T(8,128)} %get-tuple-element.6, f32[32]{0:T(128)S(1)} %get-tuple-element.8, f32[512,32]{0,1:T(8,128)S(1)} %copy-done, f32[512,32]{0,1:T(8,128)S(1)} %copy-done.1), kind=kLoop, calls=%fused_computation | loop fusion | flops 65536 | bytes 327936 | tf_op jit(solution)/shard_map/transpose | solution.py:437
  104.0 0.0 copy-done.2
  104.0 0.7 multiply_add_fusion
Async XLA Ops:
  0.6 101.7 %copy-start = (f32[512,32]{0,1:T(8,128)S(1)}, f32[512,32]{0,1:T(8,128)}, u32[]{:S(2)}) copy-start(f32[512,32]{0,1:T(8,128)} %param.11) | copy-start | bytes 196612
  0.6 101.7 %copy-start.1 = (f32[512,32]{0,1:T(8,128)S(1)}, f32[512,32]{0,1:T(8,128)}, u32[]{:S(2)}) copy-start(f32[512,32]{0,1:T(8,128)} %param.10) | copy-start | bytes 196612
  102.4 1.6 %copy-start.2 = (f32[512,32]{0,1:T(8,128)S(1)}, f32[512,32]{0,1:T(8,128)}, u32[]{:S(2)}) copy-start(f32[512,32]{0,1:T(8,128)} %param.9) | copy-start | bytes 196612

commit v5 on v4

--- a/solution.py
+++ b/solution.py
@@ -230,11 +230,12 @@
 
     def arrived(j):
         gather_col(j).wait_recv()
-        gcol[j, SENT:, :] = gcol[j, FEATS:MISC, :]
 
         @pl.when(lax.rem(j, 2) == 0)
         def _():
             forward(j).start()
+
+        gcol[j, SENT:, :] = gcol[j, FEATS:MISC, :]
 
     arrived(HALF + 4)
     distances(v0, 0, HALF + 4, 0)

time: 105 us -> 105 us (level)
  no operation moved by 1% of the time
where the time goes in v5:
time: 105 us
  Pallas kernels  101 us (96%)
  other arithmetic  2.3 us (2%)
    pallas_call x1, Pallas kernels, per_device(): pl.pallas_call(step_kernel, out_shape=[out, jax.ShapeDtypeStruct((probes,...  101 us

profile of v5, /device:TPU:1, one launch (start us, length us, event | category | flops | bytes accessed | tf_op | source)
XLA Modules:
  0.0 104.8 jit_solution(3512445210304155932)
XLA Ops:
  0.6 0.0 copy-start
  0.6 0.0 copy-start.1
  0.7 100.8 %cg_step.1 = (f32[32,512]{1,0:T(8,128)}, f32[32,128]{1,0:T(8,128)}) custom-call(f32[32,512]{1,0:T(8,128)} %bitcast.14, f32[1,32]{1,0:T(1,128)} %bitcast.16, s32[1,512]{1,0:T(1,128)} %bitcast.15, f32[32,512]{1,0:T(8,128)} %bitcast.13, f32[32,512]{1,0:T(8,128)} %bitcast.12), custom_call_target="tpu_custom_call" | custom-call | tf_op jit(solution)/shard_map/cg_step/pallas_call | solution.py:401
  101.5 1.0 slice_reduce_fusion
  102.4 0.0 copy-done
  102.4 0.0 copy-done.1
  102.4 0.0 copy-start.2
  102.5 1.6 %add_bitcast_fusion = (f32[512,32]{0,1:T(8,128)}, f32[512,32]{0,1:T(8,128)}) fusion(f32[32]{0:T(128)S(1)} %get-tuple-element.7, f32[32,512]{1,0:T(8,128)} %get-tuple-element.6, f32[32]{0:T(128)S(1)} %get-tuple-element.8, f32[512,32]{0,1:T(8,128)S(1)} %copy-done, f32[512,32]{0,1:T(8,128)S(1)} %copy-done.1), kind=kLoop, calls=%fused_computation | loop fusion | flops 65536 | bytes 327936 | tf_op jit(solution)/shard_map/transpose | solution.py:438
  104.1 0.0 copy-done.2
  104.1 0.7 multiply_add_fusion
Async XLA Ops:
  0.6 101.8 %copy-start = (f32[512,32]{0,1:T(8,128)S(1)}, f32[512,32]{0,1:T(8,128)}, u32[]{:S(2)}) copy-start(f32[512,32]{0,1:T(8,128)} %param.11) | copy-start | bytes 196612
  0.6 101.8 %copy-start.1 = (f32[512,32]{0,1:T(8,128)S(1)}, f32[512,32]{0,1:T(8,128)}, u32[]{:S(2)}) copy-start(f32[512,32]{0,1:T(8,128)} %param.10) | copy-start | bytes 196612
  102.4 1.6 %copy-start.2 = (f32[512,32]{0,1:T(8,128)S(1)}, f32[512,32]{0,1:T(8,128)}, u32[]{:S(2)}) copy-start(f32[512,32]{0,1:T(8,128)} %param.9) | copy-start | bytes 196612
